TPU v7x, 256 devices: a whole 4x4x8 slice. The times are simulated.
256 devices in a mesh: fsdp: 32 (over z, y_hi, core), tp: 8 (over y_lo, x).
Axes of the slice: x: 4, y: 4 (y_hi: 2, y_lo: 2; y = y_hi * 2 + y_lo), z: 8, core: 2. Of those that a mesh axis runs over, the one named last changes fastest.
Arguments:
- train_x: bfloat16 [32768, 8192], P('fsdp'), may hold values from -6 to 6
- train_q: bfloat16 [32768, 8192], P('fsdp', 'tp'), may hold values from -17 to 17
- train_k: bfloat16 [32768, 1024], P('fsdp', 'tp'), may hold values from -14 to 14
- train_target: bfloat16 [32768, 8192], P('fsdp', 'tp'), may hold values from -6 to 6
- train_skill: int32 [128], replicated, may hold values from 0 to 3, as said below
- value_weight: bfloat16 [8192, 1024], P('fsdp', 'tp'), may hold values from -0.0625 to 0.0625
- val_x: bfloat16 [4096, 8192], P('fsdp'), may hold values from -6 to 6
- val_q: bfloat16 [4096, 8192], P('fsdp', 'tp'), may hold values from -17 to 17
- val_k: bfloat16 [4096, 1024], P('fsdp', 'tp'), may hold values from -14 to 14
- val_target: bfloat16 [4096, 8192], P('fsdp', 'tp'), may hold values from -6 to 6
- val_skill: int32 [32], replicated, may hold values from 0 to 3, as said below
Outputs:
- skill_grads: bfloat16 [4, 8192, 1024], P(None, 'fsdp', 'tp')
- transfer: float32 [4, 4], replicated
Inputs may be any that keep to these rules, and one draw needn't show every extreme that they name: `train_skill`: each of the 4 skills labels exactly 32 sequences. `val_skill`: each of the 4 skills labels exactly 8 sequences.
All inputs are finite; a program needn't handle non-finite values.
Results may differ from a plain program's by a relative error of at most 0.0052.
The roundings to bfloat16 on the way count: a program that leaves them out, or rounds other values in their place, can miss the bound.
Values may be sent and summed in bfloat16 or wider, within the bound.
No kernel may reach another device: no remote copies, remote signals or barrier semaphores. Data moves between devices by JAX's collectives and lax.ppermute only.
A program may use at most 192 MiB of HBM per device.

v0:
```python
import math
import jax
import jax.numpy as jnp
from jax import lax
from jax.sharding import PartitionSpec as P

HD = 128
SKILLS = 4
SEQ = 256
VSEQ = 128
step_size = 0.01


def attend(query_rows, key_rows, length):
    members = query_rows.shape[0] // length
    kv_heads = key_rows.shape[1] // HD
    group = query_rows.shape[1] // HD // kv_heads
    queries = query_rows.reshape(members, length, kv_heads, group, HD)
    keys = key_rows.reshape(members, length, kv_heads, HD)
    scores = jnp.einsum("bqgrh,bkgh->bgrqk", queries, keys, preferred_element_type=jnp.float32) * (
        1.0 / math.sqrt(HD)
    )
    places = jnp.arange(length)
    allowed = places[:, None] >= places[None, :]
    scores = jnp.where(allowed, scores, jnp.float32(-1e30))
    highest = jnp.max(scores, axis=-1, keepdims=True)
    raised = jnp.exp(scores - highest)
    return (raised / jnp.sum(raised, axis=-1, keepdims=True)).astype(jnp.bfloat16)


def on_device(
    train_x,
    train_q,
    train_k,
    train_target,
    train_skill,
    value_weight,
    val_x,
    val_q,
    val_k,
    val_target,
    val_skill,
):
    head_width = train_k.shape[1]
    kv_heads = head_width // HD
    group = train_q.shape[1] // head_width
    train_rows = train_x.shape[0]
    val_rows = val_x.shape[0]
    train_members = train_rows // SEQ
    val_members = val_rows // VSEQ
    skill_ids = jnp.arange(SKILLS, dtype=jnp.int32)
    shard_rows = lax.all_gather(value_weight, "fsdp", axis=0, tiled=True)
    values = jnp.dot(train_x, shard_rows, preferred_element_type=jnp.float32)
    val_values = jnp.dot(val_x, shard_rows, preferred_element_type=jnp.float32)
    values = values.astype(jnp.bfloat16)
    val_values = val_values.astype(jnp.bfloat16)
    attention = attend(train_q, train_k, SEQ)
    value_blocks = values.reshape(train_members, SEQ, kv_heads, HD)
    mixed = jnp.einsum(
        "bgrqk,bkgh->bqgrh", attention, value_blocks, preferred_element_type=jnp.float32
    )
    target_blocks = train_target.reshape(train_members, SEQ, kv_heads, group, HD).astype(
        jnp.float32
    )
    residual = ((mixed - target_blocks) / SEQ).astype(jnp.bfloat16)
    value_grads = jnp.einsum(
        "bgrqk,bqgrh->bkgh", attention, residual, preferred_element_type=jnp.float32
    )
    grad_rows = value_grads.reshape(train_rows, head_width).astype(jnp.bfloat16)
    train_first = lax.axis_index("fsdp") * train_members
    local_skill = lax.dynamic_slice_in_dim(train_skill, train_first, train_members)
    local_indicator = (local_skill[:, None] == skill_ids[None, :]).astype(jnp.float32)
    running = jnp.zeros(
        (lax.axis_size("fsdp") * (train_x.shape[1] // lax.axis_size("fsdp")), SKILLS, head_width),
        jnp.float32,
    )
    for sequence in range(train_members):
        product = jnp.dot(
            train_x[sequence * SEQ : (sequence + 1) * SEQ].T,
            grad_rows[sequence * SEQ : (sequence + 1) * SEQ],
            preferred_element_type=jnp.float32,
        )
        running = running + local_indicator[sequence][None, :, None] * product[:, None, :]
    shares = lax.psum_scatter(running, "fsdp", scatter_dimension=0, tiled=True)
    skill_grads = jnp.transpose(shares, (1, 0, 2)).astype(jnp.bfloat16)
    val_attention = attend(val_q, val_k, VSEQ)
    val_blocks = val_values.reshape(val_members, VSEQ, kv_heads, HD)
    val_mixed = jnp.einsum(
        "bgrqk,bkgh->bqgrh", val_attention, val_blocks, preferred_element_type=jnp.float32
    )
    val_target_blocks = val_target.reshape(val_members, VSEQ, kv_heads, group, HD).astype(
        jnp.float32
    )
    val_residual = (val_mixed - val_target_blocks) / VSEQ
    val_pull = jnp.einsum(
        "bgrqk,bqgrh->bkgh",
        val_attention.astype(jnp.float32),
        val_residual,
        precision=lax.Precision.HIGHEST,
    )
    val_pull = val_pull.reshape(val_rows, head_width)
    tangent = jnp.einsum(
        "td,sdc->tsc",
        val_x,
        lax.all_gather(skill_grads, "fsdp", axis=1, tiled=True),
        preferred_element_type=jnp.float32,
    )
    along = jnp.einsum("tsc,tc->ts", tangent, val_pull, precision=lax.Precision.HIGHEST)
    val_first = lax.axis_index("fsdp") * val_members
    val_local = lax.dynamic_slice_in_dim(val_skill, val_first, val_members)
    val_indicator = jnp.repeat(
        (val_local[:, None] == skill_ids[None, :]).astype(jnp.float32), VSEQ, axis=0
    )
    partial_transfer = step_size * jnp.dot(along.T, val_indicator, precision=lax.Precision.HIGHEST)
    transfer = lax.psum(partial_transfer, ("fsdp", "tp"))
    return (skill_grads, transfer)


def solution(mesh):
    placed = (
        P("fsdp", None),
        P("fsdp", "tp"),
        P("fsdp", "tp"),
        P("fsdp", "tp"),
        P(),
        P("fsdp", "tp"),
        P("fsdp", None),
        P("fsdp", "tp"),
        P("fsdp", "tp"),
        P("fsdp", "tp"),
        P(),
    )
    return jax.shard_map(
        on_device,
        mesh=mesh,
        in_specs=placed,
        out_specs=(P(None, "fsdp", "tp"), P()),
        check_vma=False,
    )
```

profile of v0, /device:TPU:1, one launch (start us, length us, event | category | flops | bytes accessed | tf_op | source)
XLA Modules:
  0.0 577.4 jit_solution(3521864218452400355)
XLA Ops:
  7.2 0.0 copy-start
  7.2 0.0 all-gather.3.cloned.1.call-start
  7.2 0.7 all-gather.3.cloned.1.call-update
  7.9 0.0 reduce-scatter.2.cloned.1.call-start
  8.0 3.6 copy.56
  11.5 2.0 convert_bitcast_fusion
  13.6 0.0 copy-start.6
  13.6 0.0 copy-start.4
  13.6 2.9 copy.57
  16.5 5.2 copy.28
  21.8 0.0 copy-done.6
  21.8 0.1 dynamic_slice.6
  21.9 0.1 fusion.66
  22.0 0.0 copy-done.4
  22.0 3.1 fusion.1
  25.0 0.0 copy-start.1
  25.0 3.2 copy-done.1
  28.2 1.9 fusion
  30.1 64.9 %all-gather.3.cloned.1.call-done = bf16[8192,128]{1,0:T(8,128)(2,1)} async-done(((bf16[256,128]{1,0:T(8,128)(2,1)}), bf16[8192,128]{1,0:T(8,128)(2,1)}) %all-gather.3.cloned.1.call-update) | async-done | bytes 2097168 | tf_op jit(solution)/shard_map/all_gather | solution.py:52
  95.0 10.8 %convolution_convert_fusion = bf16[1024,128]{1,0:T(8,128)(2,1)S(1)} fusion(bf16[1024,8192]{1,0:T(8,128)(2,1)} %param.11, bf16[8192,128]{1,0:T(8,128)(2,1)} %all-gather.3.cloned.1.call-done), kind=kOutput, calls=%fused_computation.35 | convolution fusion | flops 2147614720 | bytes 19136512 | tf_op jit(solution)/shard_map/dot_general | solution.py:53
  105.9 9.5 %fusion.42 = bf16[4,256,1,128]{1,3,0,2:T(8,128)(2,1)S(1)} fusion(f32[4,8,256]{2,1,0:T(8,128)S(1)} %fusion, f32[4,8,256]{2,1,0:T(8,128)S(1)} %get-tuple-element.6, f32[4,256,256,8]{2,1,3,0:T(8,128)} %copy-done.1, pred[256,256]{0,1:T(8,128)(4,1)S(1)} %iota_compare_fusion, f32[4,256,1,8,128]{1,4,3,0,2:T(8,128)} %copy.28, bf16[4,256,128,1]{2,1,3,0:T(8,128)(2,1)S(1)} %bitcast.216), kind=kOutput, calls=%fused_computation.38 | convolution fusion | flops 1097990144 | bytes 13238272 | tf_op jit(solution)/shard_map/bgrqk,bqgrh->bkgh/dot_general | solution.py:66
  115.4 4.9 convolution_bitcast_fusion
  120.3 4.9 convolution_bitcast_fusion.1
  125.2 4.9 convolution_bitcast_fusion.2
  130.1 4.8 convolution_bitcast_fusion.3
  134.9 5.6 copy.33
  140.5 5.6 copy.32
  146.1 5.6 copy.31
  151.6 5.6 copy.30
  157.2 12.5 %multiply_add_fusion = f32[8192,4,128]{2,0,1:T(8,128)} fusion(f32[8192,128]{1,0:T(8,128)} %copy.33, f32[4]{0:T(128)S(1)} %get-tuple-element.3, f32[8192,128]{1,0:T(8,128)} %copy.32, f32[4]{0:T(128)S(1)} %get-tuple-element.4, f32[8192,128]{1,0:T(8,128)} %copy.31, f32[4]{0:T(128)S(1)} %get-tuple-element.5, f32[8192,128]{1,0:T(8,128)} %copy.30, ...), kind=kLoop, calls=%fused_computation | loop fusion | flops 29360128 | bytes 33554496 | tf_op jit(solution)/shard_map/add | solution.py:83
  169.8 0.0 copy-start.5
  169.8 0.0 reduce-scatter.2.cloned.1.call-update
  169.8 0.0 all-gather.5.cloned.1.call-start
  169.9 212.2 %reduce-scatter.2.cloned.1.call-done = f32[256,4,128]{2,0,1:T(8,128)} async-done(((f32[8192,4,128]{2,0,1:T(8,128)}), f32[256,4,128]{2,0,1:T(8,128)}) %reduce-scatter.2.cloned.1.call-update) | async-done | bytes 524304 | tf_op jit(solution)/shard_map/reduce_scatter | solution.py:84
  382.1 1.8 convert_bitcast_fusion.1
  383.9 0.0 all-gather.5.cloned.1.call-update
  383.9 0.0 copy-done.2
  383.9 0.1 copy.36
  384.1 0.6 dynamic_slice.7
  384.7 0.6 compare_convert_fusion
  385.3 0.2 fusion.72
  385.6 0.1 fusion.59
  385.7 3.5 fusion.33
  389.2 1.5 convolution_bitcast_fusion.5
  390.7 99.5 %all-gather.5.cloned.1.call-done = bf16[4,8192,128]{2,1,0:T(8,128)(2,1)} async-done(((bf16[4,256,128]{2,1,0:T(8,128)(2,1)}), bf16[4,8192,128]{2,1,0:T(8,128)(2,1)}) %all-gather.5.cloned.1.call-update) | async-done | bytes 8388624 | tf_op jit(solution)/shard_map/all_gather | solution.py:105
  490.2 5.8 fusion.55
  495.9 0.2 convolution_multiply_fusion.1
  496.1 74.7 %psum.7 = f32[4,4]{1,0:T(4,128)} all-reduce(f32[4,4]{1,0:T(4,128)S(1)} %convolution_multiply_fusion.1), channel_id=1, replica_groups=mesh['fsdp'=32,'tp'=8] {'fsdp','tp'}, use_global_device_ids=true, to_apply=%region_5.6 | all-reduce | flops 16 | bytes 128 | tf_op jit(solution)/shard_map/psum | solution.py:115
  (10 shorter events, 0.1 us)
Async XLA Ops:
  7.2 378.5 %copy-start = (bf16[128,8192]{1,0:T(8,128)(2,1)S(1)}, bf16[128,8192]{1,0:T(8,128)(2,1)}, u32[]{:S(2)}) copy-start(bf16[128,8192]{1,0:T(8,128)(2,1)} %param.17) | copy-start | bytes 6291460
  7.2 87.8 %all-gather.3.cloned.1.call-start = ((), (), s32[]{:S(2)}) async-start(), calls=%async_computation.1 | async-start | bytes 2162688 | tf_op jit(solution)/shard_map/all_gather | solution.py:52
  7.9 374.2 %reduce-scatter.2.cloned.1.call-start = ((), (), s32[]{:S(2)}) async-start(), calls=%async_computation.2 | async-start | bytes 17301504 | tf_op jit(solution)/shard_map/reduce_scatter | solution.py:84
  13.6 8.2 %copy-start.6 = (s32[128]{0:T(128)S(1)}, s32[128]{0:T(128)}, u32[]{:S(2)}) copy-start(s32[128]{0:T(128)} %param.15) | copy-start | bytes 1540
  13.6 8.4 %copy-start.4 = (bf16[1024,128]{1,0:T(8,128)(2,1)S(1)}, bf16[1024,128]{1,0:T(8,128)(2,1)}, u32[]{:S(2)}) copy-start(bf16[1024,128]{1,0:T(8,128)(2,1)} %param.13) | copy-start | bytes 786436
  25.0 3.2 copy-start.1
  169.8 214.1 %copy-start.2 = (bf16[128,1024]{1,0:T(8,128)(2,1)S(1)}, bf16[128,1024]{1,0:T(8,128)(2,1)}, u32[]{:S(2)}) copy-start(bf16[128,1024]{1,0:T(8,128)(2,1)} %param.20) | copy-start | bytes 786436
  169.8 214.3 %copy-start.7 = (s32[32]{0:T(128)S(1)}, s32[32]{0:T(128)}, u32[]{:S(2)}) copy-start(s32[32]{0:T(128)} %param.21) | copy-start | bytes 388
  169.8 215.5 %copy-start.3 = (bf16[128,1024]{1,0:T(8,128)(2,1)S(1)}, bf16[128,1024]{1,0:T(8,128)(2,1)}, u32[]{:S(2)}) copy-start(bf16[128,1024]{1,0:T(8,128)(2,1)} %param.18) | copy-start | bytes 786436
  169.8 215.6 %copy-start.5 = (bf16[128,128]{1,0:T(8,128)(2,1)S(1)}, bf16[128,128]{1,0:T(8,128)(2,1)}, u32[]{:S(2)}) copy-start(bf16[128,128]{1,0:T(8,128)(2,1)} %param.19) | copy-start | bytes 98308
  169.8 320.4 %all-gather.5.cloned.1.call-start = ((), (), s32[]{:S(2)}) async-start(), calls=%async_computation.3 | async-start | bytes 8650752 | tf_op jit(solution)/shard_map/all_gather | solution.py:105
Sparse Core Ops, SparseCore 0:
  10.8 84.1 all-gather.2
  169.9 212.1 reduce-scatter.1
  385.9 104.2 all-gather.4
where the time goes:
time: 578 us; the launch traced here: 577 us
  waiting for transfers between devices  377 us (65%)
  blocking collectives  74.7 us (13%)
  matrix products  54.1 us (9%)
  local copies, waits for them, and re-layouts  38.1 us (7%)
  other arithmetic  19.1 us (3%)
  between operations  13.9 us (2%)
    reduce_scatter x1, waiting for transfers between devices, on_device(): shares = lax.psum_scatter(running, 'fsdp', scatter_dimension=0, tiled=True)  212 us
    all_gather x1, waiting for transfers between devices, on_device(): lax.all_gather(skill_grads, 'fsdp', axis=1, tiled=True)  99.5 us
    psum x1, blocking collectives, on_device(): transfer = lax.psum(partial_transfer, ('fsdp', 'tp'))  74.7 us
    all_gather x1, waiting for transfers between devices, on_device(): shard_rows = lax.all_gather(value_weight, 'fsdp', axis=0, tiled=True)  64.9 us
    dot_general x4, local copies, waits for them, and re-layouts, on_device(): jnp.dot(train_x[sequence * SEQ:(sequence + 1) * SEQ].T, grad_rows[sequenc...  22.3 us
    dot_general x4, matrix products, on_device(): jnp.dot(train_x[sequence * SEQ:(sequence + 1) * SEQ].T, grad_rows[sequenc...  19.5 us
    add x1, other arithmetic, on_device(): running + local_indicator[sequence][None, :, None] * product[:, None, :]  12.5 us
  transfers between devices with their start and end apart: 3, of which 3 were waited for; matrix products, arithmetic and copies ran while one was open for 4% of the time, Pallas kernels for 0%

commit v1 on v0

--- a/solution.py
+++ b/solution.py
@@ -102,7 +102,9 @@
     tangent = jnp.einsum(
         "td,sdc->tsc",
         val_x,
-        lax.all_gather(skill_grads, "fsdp", axis=1, tiled=True),
+        jnp.concatenate(
+            lax.all_to_all(jnp.stack([skill_grads] * lax.axis_size("fsdp")), "fsdp", 0, 0), axis=1
+        ),
         preferred_element_type=jnp.float32,
     )
     along = jnp.einsum("tsc,tc->ts", tangent, val_pull, precision=lax.Precision.HIGHEST)

time: 578 us -> 682 us (1.18)
  waiting for transfers between devices: 377 us -> 457 us
  local copies, waits for them, and re-layouts: 38.1 us -> 51.1 us
  starting transfers between devices: 0.12 us -> 11 us
    all_to_all x0 -> x1, waiting for transfers between devices: none -> 179 us  [on_device(): lax.all_to_all(jnp.stack([skill_grads] * lax.axis_size('fsdp')), 'fsdp',...]
    all_gather x1 -> x0, waiting for transfers between devices: 99.5 us -> none  [on_device(): lax.all_gather(skill_grads, 'fsdp', axis=1, tiled=True)]
    all_to_all x0 -> x1, starting transfers between devices: none -> 10.9 us  [on_device(): lax.all_to_all(jnp.stack([skill_grads] * lax.axis_size('fsdp')), 'fsdp',...]
    all_to_all x0 -> x1, local copies, waits for them, and re-layouts: none -> 7.7 us  [on_device(): lax.all_to_all(jnp.stack([skill_grads] * lax.axis_size('fsdp')), 'fsdp',...]
where the time goes in v1:
time: 682 us; the launch traced here: 681 us
  waiting for transfers between devices  457 us (67%)
  blocking collectives  74.9 us (11%)
  matrix products  54.9 us (8%)
  local copies, waits for them, and re-layouts  51.1 us (7%)
  other arithmetic  18.4 us (3%)
  between operations  14.2 us (2%)
  starting transfers between devices  11 us (2%)
    reduce_scatter x1, waiting for transfers between devices, on_device(): shares = lax.psum_scatter(running, 'fsdp', scatter_dimension=0, tiled=True)  212 us
    all_to_all x1, waiting for transfers between devices, on_device(): lax.all_to_all(jnp.stack([skill_grads] * lax.axis_size('fsdp')), 'fsdp',...  179 us
    psum x1, blocking collectives, on_device(): transfer = lax.psum(partial_transfer, ('fsdp', 'tp'))  74.9 us
    all_gather x1, waiting for transfers between devices, on_device(): shard_rows = lax.all_gather(value_weight, 'fsdp', axis=0, tiled=True)  64.9 us
    dot_general x4, local copies, waits for them, and re-layouts, on_device(): jnp.dot(train_x[sequence * SEQ:(sequence + 1) * SEQ].T, grad_rows[sequenc...  22.3 us
    dot_general x4, matrix products, on_device(): jnp.dot(train_x[sequence * SEQ:(sequence + 1) * SEQ].T, grad_rows[sequenc...  19.5 us
  transfers between devices with their start and end apart: 3, of which 3 were waited for; matrix products, arithmetic and copies ran while one was open for 4% of the time, Pallas kernels for 0%

profile of v1, /device:TPU:1, one launch (start us, length us, event | category | flops | bytes accessed | tf_op | source)
XLA Modules:
  0.0 681.4 jit_solution(4866205099298088498)
XLA Ops:
  7.2 0.0 copy-start
  7.2 0.0 all-gather.2.cloned.1.call-start
  7.2 0.7 all-gather.2.cloned.1.call-update
  7.9 0.0 reduce-scatter.2.cloned.1.call-start
  8.0 3.6 copy.75
  11.5 2.0 convert_bitcast_fusion
  13.6 0.0 copy-start.6
  13.6 0.0 copy-start.4
  13.6 2.9 copy.76
  16.5 5.2 copy.41
  21.8 0.0 copy-done.6
  21.8 0.1 dynamic_slice.6
  21.9 0.1 fusion.66
  22.0 0.0 copy-done.4
  22.0 3.1 fusion.1
  25.0 3.2 copy-done.1
  28.2 1.9 fusion
  30.1 64.9 %all-gather.2.cloned.1.call-done = bf16[8192,128]{1,0:T(8,128)(2,1)} async-done(((bf16[256,128]{1,0:T(8,128)(2,1)}), bf16[8192,128]{1,0:T(8,128)(2,1)}) %all-gather.2.cloned.1.call-update) | async-done | bytes 2097168 | tf_op jit(solution)/shard_map/all_gather | solution.py:52
  95.0 10.8 %convolution_convert_fusion = bf16[1024,128]{1,0:T(8,128)(2,1)S(1)} fusion(bf16[1024,8192]{1,0:T(8,128)(2,1)} %param.11, bf16[8192,128]{1,0:T(8,128)(2,1)} %all-gather.2.cloned.1.call-done), kind=kOutput, calls=%fused_computation.35 | convolution fusion | flops 2147614720 | bytes 19136512 | tf_op jit(solution)/shard_map/dot_general | solution.py:53
  105.9 9.5 %fusion.42 = bf16[4,256,1,128]{1,3,0,2:T(8,128)(2,1)S(1)} fusion(f32[4,8,256]{2,1,0:T(8,128)S(1)} %fusion, f32[4,8,256]{2,1,0:T(8,128)S(1)} %get-tuple-element.6, f32[4,256,256,8]{2,1,3,0:T(8,128)} %copy-done.1, pred[256,256]{0,1:T(8,128)(4,1)S(1)} %iota_compare_fusion, f32[4,256,1,8,128]{1,4,3,0,2:T(8,128)} %copy.41, bf16[4,256,128,1]{2,1,3,0:T(8,128)(2,1)S(1)} %bitcast.220), kind=kOutput, calls=%fused_computation.38 | convolution fusion | flops 1097990144 | bytes 13238272 | tf_op jit(solution)/shard_map/bgrqk,bqgrh->bkgh/dot_general | solution.py:66
  115.4 4.9 convolution_bitcast_fusion
  120.3 4.9 convolution_bitcast_fusion.1
  125.2 4.9 convolution_bitcast_fusion.2
  130.1 4.8 convolution_bitcast_fusion.3
  134.9 5.6 copy.46
  140.5 5.6 copy.45
  146.1 5.6 copy.44
  151.6 5.6 copy.43
  157.2 12.5 %multiply_add_fusion = f32[8192,4,128]{2,0,1:T(8,128)} fusion(f32[8192,128]{1,0:T(8,128)} %copy.46, f32[4]{0:T(128)S(1)} %get-tuple-element.3, f32[8192,128]{1,0:T(8,128)} %copy.45, f32[4]{0:T(128)S(1)} %get-tuple-element.4, f32[8192,128]{1,0:T(8,128)} %copy.44, f32[4]{0:T(128)S(1)} %get-tuple-element.5, f32[8192,128]{1,0:T(8,128)} %copy.43, ...), kind=kLoop, calls=%fused_computation | loop fusion | flops 29360128 | bytes 33554496 | tf_op jit(solution)/shard_map/add | solution.py:83
  169.8 0.0 reduce-scatter.2.cloned.1.call-update
  169.8 212.3 %reduce-scatter.2.cloned.1.call-done = f32[256,4,128]{2,0,1:T(8,128)} async-done(((f32[8192,4,128]{2,0,1:T(8,128)}), f32[256,4,128]{2,0,1:T(8,128)}) %reduce-scatter.2.cloned.1.call-update) | async-done | bytes 524304 | tf_op jit(solution)/shard_map/reduce_scatter | solution.py:84
  382.1 1.1 convert_bitcast_fusion.1
  383.2 0.0 copy-start.2
  383.2 5.3 stack.2
  388.5 0.0 copy-done.2
  388.5 10.9 %all-to-all-start = ((bf16[32,4,256,128]{3,2,1,0:T(8,128)(2,1)}), bf16[32,4,256,128]{3,2,1,0:T(8,128)(2,1)}, u32[]{:S(2)}, u32[]{:S(2)}) async-start(bf16[32,4,256,128]{3,2,1,0:T(8,128)(2,1)} %stack.2), calls=%async_computation.1 | async-start | bytes 16777216 | tf_op jit(solution)/shard_map/all_to_all | solution.py:106
  399.4 0.1 copy.52
  399.6 0.6 dynamic_slice.7
  400.2 0.6 compare_convert_fusion
  400.8 1.2 fusion.72
  402.1 0.1 fusion.59
  402.2 3.3 fusion.33
  405.5 1.5 convolution_bitcast_fusion.5
  406.9 179.0 %all-to-all-done = bf16[32,4,256,128]{3,2,1,0:T(8,128)(2,1)} async-done(((bf16[32,4,256,128]{3,2,1,0:T(8,128)(2,1)}), bf16[32,4,256,128]{3,2,1,0:T(8,128)(2,1)}, u32[]{:S(2)}, u32[]{:S(2)}) %all-to-all-start) | async-done | bytes 8388640 | tf_op jit(solution)/shard_map/all_to_all | solution.py:106
  586.0 7.7 %copy.47 = bf16[32,4,256,128]{3,2,0,1:T(8,128)(2,1)} copy(bf16[32,4,256,128]{3,2,1,0:T(8,128)(2,1)} %all-to-all-done) | data formatting | bytes 16777216 | tf_op jit(solution)/shard_map/all_to_all | solution.py:106
  593.7 5.8 fusion.55
  599.5 0.2 convolution_multiply_fusion.1
  599.6 74.9 %psum.7 = f32[4,4]{1,0:T(4,128)} all-reduce(f32[4,4]{1,0:T(4,128)S(1)} %convolution_multiply_fusion.1), channel_id=1, replica_groups=mesh['fsdp'=32,'tp'=8] {'fsdp','tp'}, use_global_device_ids=true, to_apply=%region_5.6 | all-reduce | flops 16 | bytes 128 | tf_op jit(solution)/shard_map/psum | solution.py:117
  (11 shorter events, 0.1 us)
Async XLA Ops:
  7.2 395.0 %copy-start = (bf16[128,8192]{1,0:T(8,128)(2,1)S(1)}, bf16[128,8192]{1,0:T(8,128)(2,1)}, u32[]{:S(2)}) copy-start(bf16[128,8192]{1,0:T(8,128)(2,1)} %param.17) | copy-start | bytes 6291460
  7.2 87.8 %all-gather.2.cloned.1.call-start = ((), (), s32[]{:S(2)}) async-start(), calls=%async_computation.2 | async-start | bytes 2162688 | tf_op jit(solution)/shard_map/all_gather | solution.py:52
  7.9 374.2 %reduce-scatter.2.cloned.1.call-start = ((), (), s32[]{:S(2)}) async-start(), calls=%async_computation.3 | async-start | bytes 17301504 | tf_op jit(solution)/shard_map/reduce_scatter | solution.py:84
  13.6 8.2 %copy-start.6 = (s32[128]{0:T(128)S(1)}, s32[128]{0:T(128)}, u32[]{:S(2)}) copy-start(s32[128]{0:T(128)} %param.15) | copy-start | bytes 1540
  13.6 8.4 %copy-start.4 = (bf16[1024,128]{1,0:T(8,128)(2,1)S(1)}, bf16[1024,128]{1,0:T(8,128)(2,1)}, u32[]{:S(2)}) copy-start(bf16[1024,128]{1,0:T(8,128)(2,1)} %param.13) | copy-start | bytes 786436
  25.0 3.2 copy-start.1
  383.2 5.3 copy-start.2
  388.5 10.9 %copy-start.3 = (bf16[128,1024]{1,0:T(8,128)(2,1)S(1)}, bf16[128,1024]{1,0:T(8,128)(2,1)}, u32[]{:S(2)}) copy-start(bf16[128,1024]{1,0:T(8,128)(2,1)} %param.20) | copy-start | bytes 786436
  388.5 11.1 %copy-start.7 = (s32[32]{0:T(128)S(1)}, s32[32]{0:T(128)}, u32[]{:S(2)}) copy-start(s32[32]{0:T(128)} %param.21) | copy-start | bytes 388
  388.5 12.4 %copy-start.5 = (bf16[128,128]{1,0:T(8,128)(2,1)S(1)}, bf16[128,128]{1,0:T(8,128)(2,1)}, u32[]{:S(2)}) copy-start(bf16[128,128]{1,0:T(8,128)(2,1)} %param.19) | copy-start | bytes 98308
  388.5 197.5 %all-to-all-start = ((bf16[32,4,256,128]{3,2,1,0:T(8,128)(2,1)}), bf16[32,4,256,128]{3,2,1,0:T(8,128)(2,1)}, u32[]{:S(2)}, u32[]{:S(2)}) async-start(bf16[32,4,256,128]{3,2,1,0:T(8,128)(2,1)} %stack.2), calls=%async_computation.1 | async-start | bytes 16777216 | tf_op jit(solution)/shard_map/all_to_all | solution.py:106
Sparse Core Ops, SparseCore 0:
  10.8 84.1 all-gather.1
  169.9 212.1 reduce-scatter.1
